TPU v7x, 512 devices: a whole 4x8x8 slice. The times are simulated.
512 devices in a mesh: row: 16 (over x, y_lo, core), col: 32 (over z, y_hi).
Axes of the slice: x: 4, y: 8 (y_hi: 4, y_lo: 2; y = y_hi * 2 + y_lo), z: 8, core: 2. Of those that a mesh axis runs over, the one named last changes fastest.
Arguments:
- eigvecs: float32 [4096, 4096], P('row', 'col'), may hold values from -6 to 6
- offsets: int32 [1], replicated, may hold values from 0 to 127
- plan: int32 [1, 30], replicated, may hold values from 0 to 31
- refl_v: float32 [32, 255, 128], P('col')
- refl_t: float32 [32, 128, 128], P('col'), as said below
Outputs:
- updated: float32 [4096, 4096], P('row', 'col')
Inputs may be any that keep to these rules, and one draw needn't show every extreme that they name: For each bank entry, I - refl_v refl_t refl_v^T is orthogonal up to rounding.
All inputs are finite; a program needn't handle non-finite values.
Results may differ from a plain program's by a relative error of at most 0.00015.
Values sent between devices are 32-bit elements; how exact they have to be, the bound alone decides.
A program may use at most 64 MiB of HBM per device.

v0:
```python
import jax
import jax.numpy as jnp
from jax import lax
from jax.sharding import PartitionSpec as P

HIGHEST = lax.Precision.HIGHEST


def from_root(value, axis, root):
    mine = lax.axis_index(axis) == root
    return lax.psum(jnp.where(mine, value, jnp.zeros_like(value)), axis)


def from_behind(value, axis, by):
    devices = lax.axis_size(axis)
    pairs = [(i, i + by) for i in range(devices) if 0 <= i + by < devices]
    return lax.ppermute(value, axis, pairs)


def apply_one(extended, row_start, vectors, factor, weight):
    span_rows = vectors.shape[0]
    block_rows = lax.dynamic_slice_in_dim(extended, row_start, span_rows, 0)
    inner_prod = jnp.dot(vectors.T, block_rows, precision=HIGHEST)
    scaled = jnp.dot(factor, inner_prod, precision=HIGHEST)
    block_rows = block_rows - weight * jnp.dot(vectors, scaled, precision=HIGHEST)
    return lax.dynamic_update_slice_in_dim(extended, block_rows, row_start, 0)


def on_device(eigvecs, offsets, plan, refl_v, refl_t):
    rows_dev = eigvecs.shape[0]
    band = refl_v.shape[2]
    span_rows = refl_v.shape[1]
    per_device = rows_dev // band
    bank_dev = refl_v.shape[0]
    row_count = lax.axis_size("row")
    my_row = lax.axis_index("row")
    sweep_count = offsets.shape[0]
    block_total = row_count * per_device - 2
    head_count = 2 * band
    padded_ids = jnp.pad(plan, ((0, 0), (0, 2)))
    my_ids = lax.dynamic_slice_in_dim(padded_ids, my_row * per_device, per_device, 1).reshape(-1)
    needed = sweep_count * per_device

    def fetch_block(index, stored):
        block_id = my_ids[index]
        owner_col = block_id // bank_dev
        owner_slot = block_id % bank_dev
        got_v, got_t = (
            from_root(refl_v[owner_slot], "col", owner_col),
            from_root(refl_t[owner_slot], "col", owner_col),
        )
        return (stored[0].at[index].set(got_v), stored[1].at[index].set(got_t))

    empty = (
        jnp.zeros((needed, span_rows, band), jnp.float32),
        jnp.zeros((needed, band, band), jnp.float32),
    )
    local_v, local_t = lax.fori_loop(0, needed, fetch_block, empty)
    tick_count = 2 * sweep_count - 2 + row_count

    def run_tick(tick, matrix):
        fetched = from_behind(matrix, "row", -1)
        lag = tick - my_row
        active = (lag >= 0) & (lag % 2 == 0) & (lag < 2 * sweep_count)
        sweep = jnp.clip(lag // 2, 0, sweep_count - 1)
        first_row = offsets[sweep]

        def process(current):
            extended = jnp.concatenate([current, fetched], 0)

            def apply_block(index, extended):
                row_start = first_row + index * band
                slot = sweep * per_device + index
                is_valid = (my_row * per_device + index < block_total).astype(jnp.float32)
                return apply_one(extended, row_start, local_v[slot], local_t[slot], is_valid)

            return lax.fori_loop(0, per_device, apply_block, extended)

        def unchanged(current):
            return jnp.concatenate([current, fetched], 0)

        extended = lax.cond(active, process, unchanged, matrix)
        returned = from_behind(extended[rows_dev:], "row", 1)
        sender_lag = lag + 1
        sender_live = (
            (my_row >= 1)
            & (sender_lag >= 0)
            & (sender_lag % 2 == 0)
            & (sender_lag < 2 * sweep_count)
        )
        matrix = extended[:rows_dev]
        new_head = jnp.where(sender_live, returned, matrix)
        return matrix.at[:head_count].set(new_head)

    return lax.fori_loop(0, tick_count, run_tick, eigvecs)


def solution(mesh):
    in_specs = (P("row", "col"), P(), P(), P("col", None, None), P("col", None, None))
    out_specs = P("row", "col")
    return jax.shard_map(
        on_device, mesh=mesh, in_specs=in_specs, out_specs=out_specs, check_vma=False
    )
```

profile of v0, /device:TPU:15, one launch (start us, length us, event | category | flops | bytes accessed | tf_op | source)
XLA Modules:
  0.0 997.5 jit_solution(11573870405648408309)
XLA Ops:
  8.3 602.7 %while.62 = (s32[]{:T(128)}, f32[2,255,128]{2,1,0:T(8,128)S(1)}, f32[2,128,128]{2,1,0:T(8,128)S(1)}, s32[2]{0:T(128)S(1)}, f32[1,255,128]{2,1,0:T(8,128)S(1)}, /...) while((s32[]{:T(128)}, f32[2,255,128]{2,1,0:T(8,128)S(1)}, ...), condition=%wide.region_4.5_spmd, body=%wide.region_0.4_spmd.sunk | while | flops 147094 | bytes 2421499 | solution.py:58
  11.6 290.2 %all-reduce.6.cloned.1.call-done = (f32[1,255,128]{2,1,0:T(8,128)}, f32[1,128,128]{2,1,0:T(8,128)}) async-done(((f32[1,255,128]{2,1,0:T(8,128)}, f32[1,128,128]{2,1,0:T(8,128)}), (f32[1,255,128]{2,1,0:T(8,128)}, f32[1,128,128]{2,1,0:T(8,128)})) %all-reduce.6.cloned.1.call-update) | async-done | bytes 196112 | tf_op jit(solution)/shard_map/while/body/eval_jaxpr/psum | solution.py:11
  301.8 1.5 select_dynamic-update-slice_fusion.4
  307.3 301.6 %all-reduce.6.cloned.1.call-done = (f32[1,255,128]{2,1,0:T(8,128)}, f32[1,128,128]{2,1,0:T(8,128)}) async-done(((f32[1,255,128]{2,1,0:T(8,128)}, f32[1,128,128]{2,1,0:T(8,128)}), (f32[1,255,128]{2,1,0:T(8,128)}, f32[1,128,128]{2,1,0:T(8,128)})) %all-reduce.6.cloned.1.call-update) | async-done | bytes 196112 | tf_op jit(solution)/shard_map/while/body/eval_jaxpr/psum | solution.py:11
  609.0 1.5 select_dynamic-update-slice_fusion.4
  611.1 378.9 %while.63 = (s32[]{:T(128)}, f32[256,128]{1,0:T(8,128)S(1)}, s32[]{:T(128)}, pred[]{:T(512)}, s32[1]{0:T(128)}, /*index=5*/f32[2,255,128]{2,1,0:T(8,128)S(1)}, f...) while((s32[]{:T(128)}, f32[256,128]{1,0:T(8,128)S(1)}, s32[]{:T(128)}, pred[]{:T(512)}, ...), condition=%wide.region_10.11_spmd, body=%wide.region_5.10_spmd.sunk | while | flops 125599528 | bytes 3472517 | solution.py:95
  611.1 23.0 %collective-permute-start = (f32[256,128]{1,0:T(8,128)S(1)}, f32[256,128]{1,0:T(8,128)S(1)}, u32[]{:S(2)}, u32[]{:S(2)}) collective-permute-start(f32[256,128]{1,0:T(8,128)S(1)} %get-tuple-element.970), channel_id=1, source_target_pairs={{32,0},{64,32},{96,64},{128,96},{160,128},{192,160},{224,192},{256... | collective-permute-start | bytes 393224 | tf_op jit(solution)/shard_map/while/body/eval_jaxpr/ppermute | solution.py:17
  634.2 0.9 collective-permute-done
  636.8 1.3 collective-permute-start.1
  638.1 3.0 collective-permute-done.1
  642.0 5.6 collective-permute-start
  647.6 0.9 collective-permute-done
  650.2 1.3 collective-permute-start.1
  651.5 3.0 collective-permute-done.1
  655.4 5.6 collective-permute-start
  663.6 1.3 collective-permute-start.1
  665.0 3.0 collective-permute-done.1
  668.9 5.6 collective-permute-start
  677.1 1.3 collective-permute-start.1
  678.4 3.0 collective-permute-done.1
  682.3 6.4 collective-permute-start
  691.3 1.3 collective-permute-start.1
  692.6 3.0 collective-permute-done.1
  696.5 6.5 collective-permute-start
  705.6 1.3 collective-permute-start.1
  707.0 3.0 collective-permute-done.1
  710.9 6.5 collective-permute-start
  720.0 1.3 collective-permute-start.1
  721.3 3.0 collective-permute-done.1
  725.2 6.5 collective-permute-start
  734.3 1.3 collective-permute-start.1
  735.6 3.0 collective-permute-done.1
  739.5 6.5 collective-permute-start
  748.6 1.3 collective-permute-start.1
  749.9 9.7 collective-permute-done.1
  760.5 17.9 %collective-permute-start = (f32[256,128]{1,0:T(8,128)S(1)}, f32[256,128]{1,0:T(8,128)S(1)}, u32[]{:S(2)}, u32[]{:S(2)}) collective-permute-start(f32[256,128]{1,0:T(8,128)S(1)} %get-tuple-element.970), channel_id=1, source_target_pairs={{32,0},{64,32},{96,64},{128,96},{160,128},{192,160},{224,192},{256... | collective-permute-start | bytes 393224 | tf_op jit(solution)/shard_map/while/body/eval_jaxpr/ppermute | solution.py:17
  781.1 1.3 collective-permute-start.1
  782.4 11.7 %collective-permute-done.1 = f32[256,128]{1,0:T(8,128)S(1)} collective-permute-done((f32[256,128]{1,0:T(8,128)S(1)}, f32[256,128]{1,0:T(8,128)S(1)}, u32[]{:S(2)}, u32[]{:S(2)}) %collective-permute-start.1) | collective-permute-done | bytes 131104 | tf_op jit(solution)/shard_map/while/body/eval_jaxpr/ppermute | solution.py:17
  795.0 17.8 %collective-permute-start = (f32[256,128]{1,0:T(8,128)S(1)}, f32[256,128]{1,0:T(8,128)S(1)}, u32[]{:S(2)}, u32[]{:S(2)}) collective-permute-start(f32[256,128]{1,0:T(8,128)S(1)} %get-tuple-element.970), channel_id=1, source_target_pairs={{32,0},{64,32},{96,64},{128,96},{160,128},{192,160},{224,192},{256... | collective-permute-start | bytes 393224 | tf_op jit(solution)/shard_map/while/body/eval_jaxpr/ppermute | solution.py:17
  815.4 1.3 collective-permute-start.1
  816.7 11.9 %collective-permute-done.1 = f32[256,128]{1,0:T(8,128)S(1)} collective-permute-done((f32[256,128]{1,0:T(8,128)S(1)}, f32[256,128]{1,0:T(8,128)S(1)}, u32[]{:S(2)}, u32[]{:S(2)}) %collective-permute-start.1) | collective-permute-done | bytes 131104 | tf_op jit(solution)/shard_map/while/body/eval_jaxpr/ppermute | solution.py:17
  829.6 17.4 %collective-permute-start = (f32[256,128]{1,0:T(8,128)S(1)}, f32[256,128]{1,0:T(8,128)S(1)}, u32[]{:S(2)}, u32[]{:S(2)}) collective-permute-start(f32[256,128]{1,0:T(8,128)S(1)} %get-tuple-element.970), channel_id=1, source_target_pairs={{32,0},{64,32},{96,64},{128,96},{160,128},{192,160},{224,192},{256... | collective-permute-start | bytes 393224 | tf_op jit(solution)/shard_map/while/body/eval_jaxpr/ppermute | solution.py:17
  849.6 1.3 collective-permute-start.1
  850.9 12.2 %collective-permute-done.1 = f32[256,128]{1,0:T(8,128)S(1)} collective-permute-done((f32[256,128]{1,0:T(8,128)S(1)}, f32[256,128]{1,0:T(8,128)S(1)}, u32[]{:S(2)}, u32[]{:S(2)}) %collective-permute-start.1) | collective-permute-done | bytes 131104 | tf_op jit(solution)/shard_map/while/body/eval_jaxpr/ppermute | solution.py:17
  864.0 17.2 %collective-permute-start = (f32[256,128]{1,0:T(8,128)S(1)}, f32[256,128]{1,0:T(8,128)S(1)}, u32[]{:S(2)}, u32[]{:S(2)}) collective-permute-start(f32[256,128]{1,0:T(8,128)S(1)} %get-tuple-element.970), channel_id=1, source_target_pairs={{32,0},{64,32},{96,64},{128,96},{160,128},{192,160},{224,192},{256... | collective-permute-start | bytes 393224 | tf_op jit(solution)/shard_map/while/body/eval_jaxpr/ppermute | solution.py:17
  883.9 1.3 collective-permute-start.1
  885.2 12.5 %collective-permute-done.1 = f32[256,128]{1,0:T(8,128)S(1)} collective-permute-done((f32[256,128]{1,0:T(8,128)S(1)}, f32[256,128]{1,0:T(8,128)S(1)}, u32[]{:S(2)}, u32[]{:S(2)}) %collective-permute-start.1) | collective-permute-done | bytes 131104 | tf_op jit(solution)/shard_map/while/body/eval_jaxpr/ppermute | solution.py:17
  898.6 16.8 %collective-permute-start = (f32[256,128]{1,0:T(8,128)S(1)}, f32[256,128]{1,0:T(8,128)S(1)}, u32[]{:S(2)}, u32[]{:S(2)}) collective-permute-start(f32[256,128]{1,0:T(8,128)S(1)} %get-tuple-element.970), channel_id=1, source_target_pairs={{32,0},{64,32},{96,64},{128,96},{160,128},{192,160},{224,192},{256... | collective-permute-start | bytes 393224 | tf_op jit(solution)/shard_map/while/body/eval_jaxpr/ppermute | solution.py:17
  918.1 1.3 collective-permute-start.1
  919.4 12.7 %collective-permute-done.1 = f32[256,128]{1,0:T(8,128)S(1)} collective-permute-done((f32[256,128]{1,0:T(8,128)S(1)}, f32[256,128]{1,0:T(8,128)S(1)}, u32[]{:S(2)}, u32[]{:S(2)}) %collective-permute-start.1) | collective-permute-done | bytes 131104 | tf_op jit(solution)/shard_map/while/body/eval_jaxpr/ppermute | solution.py:17
  933.1 16.7 %collective-permute-start = (f32[256,128]{1,0:T(8,128)S(1)}, f32[256,128]{1,0:T(8,128)S(1)}, u32[]{:S(2)}, u32[]{:S(2)}) collective-permute-start(f32[256,128]{1,0:T(8,128)S(1)} %get-tuple-element.970), channel_id=1, source_target_pairs={{32,0},{64,32},{96,64},{128,96},{160,128},{192,160},{224,192},{256... | collective-permute-start | bytes 393224 | tf_op jit(solution)/shard_map/while/body/eval_jaxpr/ppermute | solution.py:17
  952.4 1.3 collective-permute-start.1
  953.7 13.0 %collective-permute-done.1 = f32[256,128]{1,0:T(8,128)S(1)} collective-permute-done((f32[256,128]{1,0:T(8,128)S(1)}, f32[256,128]{1,0:T(8,128)S(1)}, u32[]{:S(2)}, u32[]{:S(2)}) %collective-permute-start.1) | collective-permute-done | bytes 131104 | tf_op jit(solution)/shard_map/while/body/eval_jaxpr/ppermute | solution.py:17
  967.7 5.5 collective-permute-start
  974.1 10.8 %conditional.2 = (f32[512,128]{1,0:T(8,128)}) conditional(s32[]{:T(128)} %convert_element_type.21, (f32[256,128]{1,0:T(8,128)S(1)}, f32[256,128]{1,0:T(8,128)S(1)}) %tuple.149, (f32[256,128]{1,0:T(8,128)S(1)}, f32[256,128]{1,0:T(8,128)S(1)}, s32[1]{0:T(128)}, s32[]{:T(128)}, s32[]{:T(128)}, /*index=5*/s32[]{:T(128)}, pred[]{:T(512)}, ...), branch_computations={%region_6.6_spmd, %region_7.9_spmd} | conditional | flops 125566744 | bytes 1767995 | solution.py:82
  974.8 10.1 %while.61 = (s32[]{:T(128)}, f32[512,128]{1,0:T(8,128)}, s32[]{:T(128)}, s32[]{:T(128)}, s32[]{:T(128)}, /*index=5*/f32[2,255,128]{2,1,0:T(8,128)S(1)}, f32[2,12...) while((s32[]{:T(128)}, f32[512,128]{1,0:T(8,128)}, ...), condition=%wide.region_9.8_spmd, body=%wide.region_8.7_spmd.sunk | while | flops 125501192 | bytes 1243419 | solution.py:77
  975.5 1.3 fusion.30
  977.0 1.2 fusion.32
  978.2 1.7 dynamic_update_slice.10
  980.5 1.3 fusion.30
  982.1 1.2 fusion.32
  983.2 1.6 dynamic_update_slice.10
  985.8 1.3 collective-permute-start.1
  987.1 1.9 collective-permute-done.1
  (113 shorter events, 74.0 us)
Async XLA Ops:
  6.5 0.9 copy-start.4
  6.5 0.7 copy-start.6
  7.5 0.8 copy-start.3
  7.5 0.8 copy-start.5
  8.3 602.8 %copy-start.1 = (f32[256,128]{1,0:T(8,128)S(1)}, f32[256,128]{1,0:T(8,128)}, u32[]{:S(2)}) copy-start(f32[256,128]{1,0:T(8,128)} %param.21) | copy-start | bytes 393220
  8.3 293.5 %all-reduce.6.cloned.1.call-start = ((), (), s32[]{:S(2)}) async-start(), calls=%async_computation | async-start | bytes 393216 | tf_op jit(solution)/shard_map/while/body/eval_jaxpr/psum | solution.py:11
  301.8 1.5 copy-start.2
  304.0 305.0 %all-reduce.6.cloned.1.call-start = ((), (), s32[]{:S(2)}) async-start(), calls=%async_computation | async-start | bytes 393216 | tf_op jit(solution)/shard_map/while/body/eval_jaxpr/psum | solution.py:11
  609.0 1.5 copy-start.2
  611.1 24.0 %collective-permute-start = (f32[256,128]{1,0:T(8,128)S(1)}, f32[256,128]{1,0:T(8,128)S(1)}, u32[]{:S(2)}, u32[]{:S(2)}) collective-permute-start(f32[256,128]{1,0:T(8,128)S(1)} %get-tuple-element.970), channel_id=1, source_target_pairs={{32,0},{64,32},{96,64},{128,96},{160,128},{192,160},{224,192},{256... | collective-permute-start | bytes 393224 | tf_op jit(solution)/shard_map/while/body/eval_jaxpr/ppermute | solution.py:17
  636.8 4.3 collective-permute-start.1
  642.0 6.6 collective-permute-start
  650.2 4.3 collective-permute-start.1
  655.4 6.6 collective-permute-start
  663.6 4.3 collective-permute-start.1
  668.9 6.6 collective-permute-start
  677.1 4.3 collective-permute-start.1
  682.3 7.4 collective-permute-start
  691.3 4.3 collective-permute-start.1
  696.5 7.5 collective-permute-start
  705.6 4.3 collective-permute-start.1
  710.9 7.5 collective-permute-start
  720.0 4.3 collective-permute-start.1
  725.2 7.5 collective-permute-start
  734.3 4.3 collective-permute-start.1
  739.5 7.5 collective-permute-start
  748.6 11.0 %collective-permute-start.1 = (f32[256,128]{1,0:T(8,128)S(1)}, f32[256,128]{1,0:T(8,128)S(1)}, u32[]{:S(2)}, u32[]{:S(2)}) collective-permute-start(f32[256,128]{1,0:T(8,128)S(1)} %slice.110), channel_id=1, source_target_pairs={{0,32},{32,64},{64,96},{96,128},{128,160},{160,192},{192,224},{224... | collective-permute-start | bytes 393224 | tf_op jit(solution)/shard_map/while/body/eval_jaxpr/ppermute | solution.py:17
  760.5 18.9 %collective-permute-start = (f32[256,128]{1,0:T(8,128)S(1)}, f32[256,128]{1,0:T(8,128)S(1)}, u32[]{:S(2)}, u32[]{:S(2)}) collective-permute-start(f32[256,128]{1,0:T(8,128)S(1)} %get-tuple-element.970), channel_id=1, source_target_pairs={{32,0},{64,32},{96,64},{128,96},{160,128},{192,160},{224,192},{256... | collective-permute-start | bytes 393224 | tf_op jit(solution)/shard_map/while/body/eval_jaxpr/ppermute | solution.py:17
  781.1 13.0 %collective-permute-start.1 = (f32[256,128]{1,0:T(8,128)S(1)}, f32[256,128]{1,0:T(8,128)S(1)}, u32[]{:S(2)}, u32[]{:S(2)}) collective-permute-start(f32[256,128]{1,0:T(8,128)S(1)} %slice.110), channel_id=1, source_target_pairs={{0,32},{32,64},{64,96},{96,128},{128,160},{160,192},{192,224},{224... | collective-permute-start | bytes 393224 | tf_op jit(solution)/shard_map/while/body/eval_jaxpr/ppermute | solution.py:17
  795.0 18.8 %collective-permute-start = (f32[256,128]{1,0:T(8,128)S(1)}, f32[256,128]{1,0:T(8,128)S(1)}, u32[]{:S(2)}, u32[]{:S(2)}) collective-permute-start(f32[256,128]{1,0:T(8,128)S(1)} %get-tuple-element.970), channel_id=1, source_target_pairs={{32,0},{64,32},{96,64},{128,96},{160,128},{192,160},{224,192},{256... | collective-permute-start | bytes 393224 | tf_op jit(solution)/shard_map/while/body/eval_jaxpr/ppermute | solution.py:17
  815.4 13.3 %collective-permute-start.1 = (f32[256,128]{1,0:T(8,128)S(1)}, f32[256,128]{1,0:T(8,128)S(1)}, u32[]{:S(2)}, u32[]{:S(2)}) collective-permute-start(f32[256,128]{1,0:T(8,128)S(1)} %slice.110), channel_id=1, source_target_pairs={{0,32},{32,64},{64,96},{96,128},{128,160},{160,192},{192,224},{224... | collective-permute-start | bytes 393224 | tf_op jit(solution)/shard_map/while/body/eval_jaxpr/ppermute | solution.py:17
  829.6 18.3 %collective-permute-start = (f32[256,128]{1,0:T(8,128)S(1)}, f32[256,128]{1,0:T(8,128)S(1)}, u32[]{:S(2)}, u32[]{:S(2)}) collective-permute-start(f32[256,128]{1,0:T(8,128)S(1)} %get-tuple-element.970), channel_id=1, source_target_pairs={{32,0},{64,32},{96,64},{128,96},{160,128},{192,160},{224,192},{256... | collective-permute-start | bytes 393224 | tf_op jit(solution)/shard_map/while/body/eval_jaxpr/ppermute | solution.py:17
  849.6 13.5 %collective-permute-start.1 = (f32[256,128]{1,0:T(8,128)S(1)}, f32[256,128]{1,0:T(8,128)S(1)}, u32[]{:S(2)}, u32[]{:S(2)}) collective-permute-start(f32[256,128]{1,0:T(8,128)S(1)} %slice.110), channel_id=1, source_target_pairs={{0,32},{32,64},{64,96},{96,128},{128,160},{160,192},{192,224},{224... | collective-permute-start | bytes 393224 | tf_op jit(solution)/shard_map/while/body/eval_jaxpr/ppermute | solution.py:17
  864.0 18.2 %collective-permute-start = (f32[256,128]{1,0:T(8,128)S(1)}, f32[256,128]{1,0:T(8,128)S(1)}, u32[]{:S(2)}, u32[]{:S(2)}) collective-permute-start(f32[256,128]{1,0:T(8,128)S(1)} %get-tuple-element.970), channel_id=1, source_target_pairs={{32,0},{64,32},{96,64},{128,96},{160,128},{192,160},{224,192},{256... | collective-permute-start | bytes 393224 | tf_op jit(solution)/shard_map/while/body/eval_jaxpr/ppermute | solution.py:17
  883.9 13.8 %collective-permute-start.1 = (f32[256,128]{1,0:T(8,128)S(1)}, f32[256,128]{1,0:T(8,128)S(1)}, u32[]{:S(2)}, u32[]{:S(2)}) collective-permute-start(f32[256,128]{1,0:T(8,128)S(1)} %slice.110), channel_id=1, source_target_pairs={{0,32},{32,64},{64,96},{96,128},{128,160},{160,192},{192,224},{224... | collective-permute-start | bytes 393224 | tf_op jit(solution)/shard_map/while/body/eval_jaxpr/ppermute | solution.py:17
  898.6 17.8 %collective-permute-start = (f32[256,128]{1,0:T(8,128)S(1)}, f32[256,128]{1,0:T(8,128)S(1)}, u32[]{:S(2)}, u32[]{:S(2)}) collective-permute-start(f32[256,128]{1,0:T(8,128)S(1)} %get-tuple-element.970), channel_id=1, source_target_pairs={{32,0},{64,32},{96,64},{128,96},{160,128},{192,160},{224,192},{256... | collective-permute-start | bytes 393224 | tf_op jit(solution)/shard_map/while/body/eval_jaxpr/ppermute | solution.py:17
  918.1 14.1 %collective-permute-start.1 = (f32[256,128]{1,0:T(8,128)S(1)}, f32[256,128]{1,0:T(8,128)S(1)}, u32[]{:S(2)}, u32[]{:S(2)}) collective-permute-start(f32[256,128]{1,0:T(8,128)S(1)} %slice.110), channel_id=1, source_target_pairs={{0,32},{32,64},{64,96},{96,128},{128,160},{160,192},{192,224},{224... | collective-permute-start | bytes 393224 | tf_op jit(solution)/shard_map/while/body/eval_jaxpr/ppermute | solution.py:17
  933.1 17.7 %collective-permute-start = (f32[256,128]{1,0:T(8,128)S(1)}, f32[256,128]{1,0:T(8,128)S(1)}, u32[]{:S(2)}, u32[]{:S(2)}) collective-permute-start(f32[256,128]{1,0:T(8,128)S(1)} %get-tuple-element.970), channel_id=1, source_target_pairs={{32,0},{64,32},{96,64},{128,96},{160,128},{192,160},{224,192},{256... | collective-permute-start | bytes 393224 | tf_op jit(solution)/shard_map/while/body/eval_jaxpr/ppermute | solution.py:17
  952.4 14.4 %collective-permute-start.1 = (f32[256,128]{1,0:T(8,128)S(1)}, f32[256,128]{1,0:T(8,128)S(1)}, u32[]{:S(2)}, u32[]{:S(2)}) collective-permute-start(f32[256,128]{1,0:T(8,128)S(1)} %slice.110), channel_id=1, source_target_pairs={{0,32},{32,64},{64,96},{96,128},{128,160},{160,192},{192,224},{224... | collective-permute-start | bytes 393224 | tf_op jit(solution)/shard_map/while/body/eval_jaxpr/ppermute | solution.py:17
  967.7 6.4 collective-permute-start
  985.8 3.2 collective-permute-start.1
  990.0 0.7 copy-start
Sparse Core Ops, SparseCore 0:
  12.1 289.6 all-reduce.5
  307.8 301.1 all-reduce.5
where the time goes:
time: 999 us; the launch traced here: 997 us
  waiting for transfers between devices  716 us (72%)
  starting transfers between devices  202 us (20%)
  other arithmetic  34.5 us (3%)
  local copies, waits for them, and re-layouts  21.5 us (2%)
  between operations  13.4 us (1%)
    psum x2, waiting for transfers between devices, from_root(): return lax.psum(jnp.where(mine, value, jnp.zeros_like(value)), axis)  592 us
    ppermute x32, starting transfers between devices, from_behind(): return lax.ppermute(value, axis, pairs)  202 us
    ppermute x32, waiting for transfers between devices, from_behind(): return lax.ppermute(value, axis, pairs)  124 us
  transfers between devices with their start and end apart: 34, of which 34 were waited for; matrix products, arithmetic and copies ran while one was open for 0% of the time, Pallas kernels for 0%

commit v1 on v0

--- a/solution.py
+++ b/solution.py
@@ -6,9 +6,15 @@
 HIGHEST = lax.Precision.HIGHEST
 
 
+def gather_and_add(array, name):
+    terms = lax.all_gather(array, name, axis=0, tiled=False)
+    summed = terms.sum(axis=0)
+    return summed
+
+
 def from_root(value, axis, root):
     mine = lax.axis_index(axis) == root
-    return lax.psum(jnp.where(mine, value, jnp.zeros_like(value)), axis)
+    return gather_and_add(jnp.where(mine, value, jnp.zeros_like(value)), axis)
 
 
 def from_behind(value, axis, by):

time: 999 us -> 766 us (0.77)
  waiting for transfers between devices: 716 us -> 493 us
  starting transfers between devices: 202 us -> 183 us
    psum x2 -> x0, waiting for transfers between devices: 592 us -> none  [from_root(): return lax.psum(jnp.where(mine, value, jnp.zeros_like(value)), axis)]
    all_gather x0 -> x4, waiting for transfers between devices: none -> 369 us  [gather_and_add(): terms = lax.all_gather(array, name, axis=0, tiled=False)]
    ppermute x32, starting transfers between devices: 202 us -> 182 us  [from_behind(): return lax.ppermute(value, axis, pairs)]
  transfers between devices with their start and end apart: 34 -> 36, of which waited for: 34 -> 36; matrix products, arithmetic and copies ran while one was open for 0% -> 1% of each run, Pallas kernels for 0% -> 0%
where the time goes in v1:
time: 766 us; the launch traced here: 765 us
  waiting for transfers between devices  493 us (64%)
  starting transfers between devices  183 us (24%)
  other arithmetic  44.4 us (6%)
  local copies, waits for them, and re-layouts  21.4 us (3%)
  between operations  13.1 us (2%)
    all_gather x4, waiting for transfers between devices, gather_and_add(): terms = lax.all_gather(array, name, axis=0, tiled=False)  369 us
    ppermute x32, starting transfers between devices, from_behind(): return lax.ppermute(value, axis, pairs)  182 us
    ppermute x32, waiting for transfers between devices, from_behind(): return lax.ppermute(value, axis, pairs)  124 us
  transfers between devices with their start and end apart: 36, of which 36 were waited for; matrix products, arithmetic and copies ran while one was open for 1% of the time, Pallas kernels for 0%

profile of v1, /device:TPU:15, one launch (start us, length us, event | category | flops | bytes accessed | tf_op | source)
XLA Modules:
  0.0 764.5 jit_solution(6304886815237147952)
XLA Ops:
  8.2 389.8 %while.62 = (s32[]{:T(128)}, f32[2,255,128]{2,1,0:T(8,128)S(1)}, f32[2,128,128]{2,1,0:T(8,128)S(1)}, s32[2]{0:T(128)S(1)}, f32[1,255,128]{2,1,0:T(8,128)S(1)}, /...) while((s32[]{:T(128)}, f32[2,255,128]{2,1,0:T(8,128)S(1)}, ...), condition=%wide.region_4.5_spmd, body=%wide.region_0.4_spmd.sunk | while | flops 1617814 | bytes 26883860 | solution.py:64
  9.5 1.5 broadcast_select_fusion.5
  11.8 1.5 and_reduce_fusion.2
  13.2 86.3 %all-gather.5.cloned.1.call-done = f32[32,128,128]{2,1,0:T(8,128)} async-done(((f32[1,128,128]{2,1,0:T(8,128)}), f32[32,128,128]{2,1,0:T(8,128)}) %all-gather.5.cloned.1.call-update) | async-done | bytes 2097168 | tf_op jit(solution)/shard_map/while/body/eval_jaxpr/all_gather | solution.py:10
  99.5 1.7 reduce_sum.35
  101.9 101.8 %all-gather.3.cloned.1.call-done = f32[32,255,128]{2,1,0:T(8,128)} async-done(((f32[1,255,128]{2,1,0:T(8,128)}), f32[32,255,128]{2,1,0:T(8,128)}) %all-gather.3.cloned.1.call-update) | async-done | bytes 4177936 | tf_op jit(solution)/shard_map/while/body/eval_jaxpr/all_gather | solution.py:10
  203.7 2.4 reduce_sum.34
  208.1 1.5 broadcast_select_fusion.5
  210.3 1.5 and_reduce_fusion.2
  211.8 79.1 %all-gather.5.cloned.1.call-done = f32[32,128,128]{2,1,0:T(8,128)} async-done(((f32[1,128,128]{2,1,0:T(8,128)}), f32[32,128,128]{2,1,0:T(8,128)}) %all-gather.5.cloned.1.call-update) | async-done | bytes 2097168 | tf_op jit(solution)/shard_map/while/body/eval_jaxpr/all_gather | solution.py:10
  290.9 1.7 reduce_sum.35
  293.3 101.6 %all-gather.3.cloned.1.call-done = f32[32,255,128]{2,1,0:T(8,128)} async-done(((f32[1,255,128]{2,1,0:T(8,128)}), f32[32,255,128]{2,1,0:T(8,128)}) %all-gather.3.cloned.1.call-update) | async-done | bytes 4177936 | tf_op jit(solution)/shard_map/while/body/eval_jaxpr/all_gather | solution.py:10
  394.9 2.4 reduce_sum.34
  398.1 359.2 %while.63 = (s32[]{:T(128)}, f32[256,128]{1,0:T(8,128)S(1)}, s32[]{:T(128)}, pred[]{:T(512)}, s32[1]{0:T(128)}, /*index=5*/f32[2,255,128]{2,1,0:T(8,128)S(1)}, f...) while((s32[]{:T(128)}, f32[256,128]{1,0:T(8,128)S(1)}, s32[]{:T(128)}, pred[]{:T(512)}, ...), condition=%wide.region_10.11_spmd, body=%wide.region_5.10_spmd.sunk | while | flops 125599528 | bytes 3472517 | solution.py:101
  398.1 2.9 collective-permute-start
  403.6 1.3 collective-permute-start.1
  404.9 3.0 collective-permute-done.1
  408.8 5.6 collective-permute-start
  417.0 1.3 collective-permute-start.1
  418.3 3.0 collective-permute-done.1
  422.2 5.6 collective-permute-start
  430.4 1.3 collective-permute-start.1
  431.8 3.0 collective-permute-done.1
  435.7 5.8 collective-permute-start
  444.1 1.3 collective-permute-start.1
  445.4 3.0 collective-permute-done.1
  449.3 6.5 collective-permute-start
  458.4 1.3 collective-permute-start.1
  459.8 3.0 collective-permute-done.1
  463.7 6.5 collective-permute-start
  472.8 1.3 collective-permute-start.1
  474.1 3.0 collective-permute-done.1
  478.0 6.5 collective-permute-start
  487.1 1.3 collective-permute-start.1
  488.4 3.0 collective-permute-done.1
  492.3 6.5 collective-permute-start
  501.4 1.3 collective-permute-start.1
  502.7 3.0 collective-permute-done.1
  506.6 6.5 collective-permute-start
  515.7 1.3 collective-permute-start.1
  517.1 9.7 %collective-permute-done.1 = f32[256,128]{1,0:T(8,128)S(1)} collective-permute-done((f32[256,128]{1,0:T(8,128)S(1)}, f32[256,128]{1,0:T(8,128)S(1)}, u32[]{:S(2)}, u32[]{:S(2)}) %collective-permute-start.1) | collective-permute-done | bytes 131104 | tf_op jit(solution)/shard_map/while/body/eval_jaxpr/ppermute | solution.py:23
  527.7 17.9 %collective-permute-start = (f32[256,128]{1,0:T(8,128)S(1)}, f32[256,128]{1,0:T(8,128)S(1)}, u32[]{:S(2)}, u32[]{:S(2)}) collective-permute-start(f32[256,128]{1,0:T(8,128)S(1)} %get-tuple-element.967), channel_id=1, source_target_pairs={{32,0},{64,32},{96,64},{128,96},{160,128},{192,160},{224,192},{256... | collective-permute-start | bytes 393224 | tf_op jit(solution)/shard_map/while/body/eval_jaxpr/ppermute | solution.py:23
  549.6 11.7 %collective-permute-done.1 = f32[256,128]{1,0:T(8,128)S(1)} collective-permute-done((f32[256,128]{1,0:T(8,128)S(1)}, f32[256,128]{1,0:T(8,128)S(1)}, u32[]{:S(2)}, u32[]{:S(2)}) %collective-permute-start.1) | collective-permute-done | bytes 131104 | tf_op jit(solution)/shard_map/while/body/eval_jaxpr/ppermute | solution.py:23
  562.2 17.8 %collective-permute-start = (f32[256,128]{1,0:T(8,128)S(1)}, f32[256,128]{1,0:T(8,128)S(1)}, u32[]{:S(2)}, u32[]{:S(2)}) collective-permute-start(f32[256,128]{1,0:T(8,128)S(1)} %get-tuple-element.967), channel_id=1, source_target_pairs={{32,0},{64,32},{96,64},{128,96},{160,128},{192,160},{224,192},{256... | collective-permute-start | bytes 393224 | tf_op jit(solution)/shard_map/while/body/eval_jaxpr/ppermute | solution.py:23
  583.9 11.9 %collective-permute-done.1 = f32[256,128]{1,0:T(8,128)S(1)} collective-permute-done((f32[256,128]{1,0:T(8,128)S(1)}, f32[256,128]{1,0:T(8,128)S(1)}, u32[]{:S(2)}, u32[]{:S(2)}) %collective-permute-start.1) | collective-permute-done | bytes 131104 | tf_op jit(solution)/shard_map/while/body/eval_jaxpr/ppermute | solution.py:23
  596.8 17.4 %collective-permute-start = (f32[256,128]{1,0:T(8,128)S(1)}, f32[256,128]{1,0:T(8,128)S(1)}, u32[]{:S(2)}, u32[]{:S(2)}) collective-permute-start(f32[256,128]{1,0:T(8,128)S(1)} %get-tuple-element.967), channel_id=1, source_target_pairs={{32,0},{64,32},{96,64},{128,96},{160,128},{192,160},{224,192},{256... | collective-permute-start | bytes 393224 | tf_op jit(solution)/shard_map/while/body/eval_jaxpr/ppermute | solution.py:23
  618.1 12.2 %collective-permute-done.1 = f32[256,128]{1,0:T(8,128)S(1)} collective-permute-done((f32[256,128]{1,0:T(8,128)S(1)}, f32[256,128]{1,0:T(8,128)S(1)}, u32[]{:S(2)}, u32[]{:S(2)}) %collective-permute-start.1) | collective-permute-done | bytes 131104 | tf_op jit(solution)/shard_map/while/body/eval_jaxpr/ppermute | solution.py:23
  631.3 17.3 %collective-permute-start = (f32[256,128]{1,0:T(8,128)S(1)}, f32[256,128]{1,0:T(8,128)S(1)}, u32[]{:S(2)}, u32[]{:S(2)}) collective-permute-start(f32[256,128]{1,0:T(8,128)S(1)} %get-tuple-element.967), channel_id=1, source_target_pairs={{32,0},{64,32},{96,64},{128,96},{160,128},{192,160},{224,192},{256... | collective-permute-start | bytes 393224 | tf_op jit(solution)/shard_map/while/body/eval_jaxpr/ppermute | solution.py:23
  651.1 1.3 collective-permute-start.1
  652.5 12.5 %collective-permute-done.1 = f32[256,128]{1,0:T(8,128)S(1)} collective-permute-done((f32[256,128]{1,0:T(8,128)S(1)}, f32[256,128]{1,0:T(8,128)S(1)}, u32[]{:S(2)}, u32[]{:S(2)}) %collective-permute-start.1) | collective-permute-done | bytes 131104 | tf_op jit(solution)/shard_map/while/body/eval_jaxpr/ppermute | solution.py:23
  665.9 16.8 %collective-permute-start = (f32[256,128]{1,0:T(8,128)S(1)}, f32[256,128]{1,0:T(8,128)S(1)}, u32[]{:S(2)}, u32[]{:S(2)}) collective-permute-start(f32[256,128]{1,0:T(8,128)S(1)} %get-tuple-element.967), channel_id=1, source_target_pairs={{32,0},{64,32},{96,64},{128,96},{160,128},{192,160},{224,192},{256... | collective-permute-start | bytes 393224 | tf_op jit(solution)/shard_map/while/body/eval_jaxpr/ppermute | solution.py:23
  685.4 1.3 collective-permute-start.1
  686.7 12.8 %collective-permute-done.1 = f32[256,128]{1,0:T(8,128)S(1)} collective-permute-done((f32[256,128]{1,0:T(8,128)S(1)}, f32[256,128]{1,0:T(8,128)S(1)}, u32[]{:S(2)}, u32[]{:S(2)}) %collective-permute-start.1) | collective-permute-done | bytes 131104 | tf_op jit(solution)/shard_map/while/body/eval_jaxpr/ppermute | solution.py:23
  700.4 16.7 %collective-permute-start = (f32[256,128]{1,0:T(8,128)S(1)}, f32[256,128]{1,0:T(8,128)S(1)}, u32[]{:S(2)}, u32[]{:S(2)}) collective-permute-start(f32[256,128]{1,0:T(8,128)S(1)} %get-tuple-element.967), channel_id=1, source_target_pairs={{32,0},{64,32},{96,64},{128,96},{160,128},{192,160},{224,192},{256... | collective-permute-start | bytes 393224 | tf_op jit(solution)/shard_map/while/body/eval_jaxpr/ppermute | solution.py:23
  721.0 13.0 %collective-permute-done.1 = f32[256,128]{1,0:T(8,128)S(1)} collective-permute-done((f32[256,128]{1,0:T(8,128)S(1)}, f32[256,128]{1,0:T(8,128)S(1)}, u32[]{:S(2)}, u32[]{:S(2)}) %collective-permute-start.1) | collective-permute-done | bytes 131104 | tf_op jit(solution)/shard_map/while/body/eval_jaxpr/ppermute | solution.py:23
  735.0 5.5 collective-permute-start
  741.4 10.8 %conditional.2 = (f32[512,128]{1,0:T(8,128)}) conditional(s32[]{:T(128)} %convert_element_type.21, (f32[256,128]{1,0:T(8,128)S(1)}, f32[256,128]{1,0:T(8,128)S(1)}) %tuple.149, (f32[256,128]{1,0:T(8,128)S(1)}, f32[256,128]{1,0:T(8,128)S(1)}, s32[1]{0:T(128)}, s32[]{:T(128)}, s32[]{:T(128)}, /*index=5*/s32[]{:T(128)}, pred[]{:T(512)}, ...), branch_computations={%region_6.6_spmd, %region_7.9_spmd} | conditional | flops 125566744 | bytes 1767995 | solution.py:88
  742.2 10.1 %while.61 = (s32[]{:T(128)}, f32[512,128]{1,0:T(8,128)}, s32[]{:T(128)}, s32[]{:T(128)}, s32[]{:T(128)}, /*index=5*/f32[2,255,128]{2,1,0:T(8,128)S(1)}, f32[2,12...) while((s32[]{:T(128)}, f32[512,128]{1,0:T(8,128)}, ...), condition=%wide.region_9.8_spmd, body=%wide.region_8.7_spmd.sunk | while | flops 125501192 | bytes 1243419 | solution.py:83
  742.8 1.3 fusion.36
  745.5 1.7 dynamic_update_slice.10
  747.9 1.3 fusion.36
  750.6 1.6 dynamic_update_slice.10
  753.2 1.3 collective-permute-start.1
  754.5 1.9 collective-permute-done.1
  (111 shorter events, 82.2 us)
Async XLA Ops:
  8.2 389.8 %copy-start.1 = (f32[256,128]{1,0:T(8,128)S(1)}, f32[256,128]{1,0:T(8,128)}, u32[]{:S(2)}) copy-start(f32[256,128]{1,0:T(8,128)} %param.21) | copy-start | bytes 393220
  8.2 91.3 %all-gather.5.cloned.1.call-start = ((), (), s32[]{:S(2)}) async-start(), calls=%async_computation.1 | async-start | bytes 2162688 | tf_op jit(solution)/shard_map/while/body/eval_jaxpr/all_gather | solution.py:10
  11.0 192.6 %all-gather.3.cloned.1.call-start = ((), (), s32[]{:S(2)}) async-start(), calls=%async_computation | async-start | bytes 4325376 | tf_op jit(solution)/shard_map/while/body/eval_jaxpr/all_gather | solution.py:10
  206.8 84.1 %all-gather.5.cloned.1.call-start = ((), (), s32[]{:S(2)}) async-start(), calls=%async_computation.1 | async-start | bytes 2162688 | tf_op jit(solution)/shard_map/while/body/eval_jaxpr/all_gather | solution.py:10
  209.6 185.3 %all-gather.3.cloned.1.call-start = ((), (), s32[]{:S(2)}) async-start(), calls=%async_computation | async-start | bytes 4325376 | tf_op jit(solution)/shard_map/while/body/eval_jaxpr/all_gather | solution.py:10
  398.1 3.9 collective-permute-start
  403.6 4.3 collective-permute-start.1
  408.8 6.6 collective-permute-start
  417.0 4.3 collective-permute-start.1
  422.2 6.6 collective-permute-start
  430.4 4.3 collective-permute-start.1
  435.7 6.8 collective-permute-start
  444.1 4.3 collective-permute-start.1
  449.3 7.5 collective-permute-start
  458.4 4.3 collective-permute-start.1
  463.7 7.5 collective-permute-start
  472.8 4.3 collective-permute-start.1
  478.0 7.5 collective-permute-start
  487.1 4.3 collective-permute-start.1
  492.3 7.5 collective-permute-start
  501.4 4.3 collective-permute-start.1
  506.6 7.5 collective-permute-start
  515.7 11.0 %collective-permute-start.1 = (f32[256,128]{1,0:T(8,128)S(1)}, f32[256,128]{1,0:T(8,128)S(1)}, u32[]{:S(2)}, u32[]{:S(2)}) collective-permute-start(f32[256,128]{1,0:T(8,128)S(1)} %slice.110), channel_id=1, source_target_pairs={{0,32},{32,64},{64,96},{96,128},{128,160},{160,192},{192,224},{224... | collective-permute-start | bytes 393224 | tf_op jit(solution)/shard_map/while/body/eval_jaxpr/ppermute | solution.py:23
  527.7 18.9 %collective-permute-start = (f32[256,128]{1,0:T(8,128)S(1)}, f32[256,128]{1,0:T(8,128)S(1)}, u32[]{:S(2)}, u32[]{:S(2)}) collective-permute-start(f32[256,128]{1,0:T(8,128)S(1)} %get-tuple-element.967), channel_id=1, source_target_pairs={{32,0},{64,32},{96,64},{128,96},{160,128},{192,160},{224,192},{256... | collective-permute-start | bytes 393224 | tf_op jit(solution)/shard_map/while/body/eval_jaxpr/ppermute | solution.py:23
  548.2 13.0 %collective-permute-start.1 = (f32[256,128]{1,0:T(8,128)S(1)}, f32[256,128]{1,0:T(8,128)S(1)}, u32[]{:S(2)}, u32[]{:S(2)}) collective-permute-start(f32[256,128]{1,0:T(8,128)S(1)} %slice.110), channel_id=1, source_target_pairs={{0,32},{32,64},{64,96},{96,128},{128,160},{160,192},{192,224},{224... | collective-permute-start | bytes 393224 | tf_op jit(solution)/shard_map/while/body/eval_jaxpr/ppermute | solution.py:23
  562.2 18.8 %collective-permute-start = (f32[256,128]{1,0:T(8,128)S(1)}, f32[256,128]{1,0:T(8,128)S(1)}, u32[]{:S(2)}, u32[]{:S(2)}) collective-permute-start(f32[256,128]{1,0:T(8,128)S(1)} %get-tuple-element.967), channel_id=1, source_target_pairs={{32,0},{64,32},{96,64},{128,96},{160,128},{192,160},{224,192},{256... | collective-permute-start | bytes 393224 | tf_op jit(solution)/shard_map/while/body/eval_jaxpr/ppermute | solution.py:23
  582.6 13.3 %collective-permute-start.1 = (f32[256,128]{1,0:T(8,128)S(1)}, f32[256,128]{1,0:T(8,128)S(1)}, u32[]{:S(2)}, u32[]{:S(2)}) collective-permute-start(f32[256,128]{1,0:T(8,128)S(1)} %slice.110), channel_id=1, source_target_pairs={{0,32},{32,64},{64,96},{96,128},{128,160},{160,192},{192,224},{224... | collective-permute-start | bytes 393224 | tf_op jit(solution)/shard_map/while/body/eval_jaxpr/ppermute | solution.py:23
  596.8 18.4 %collective-permute-start = (f32[256,128]{1,0:T(8,128)S(1)}, f32[256,128]{1,0:T(8,128)S(1)}, u32[]{:S(2)}, u32[]{:S(2)}) collective-permute-start(f32[256,128]{1,0:T(8,128)S(1)} %get-tuple-element.967), channel_id=1, source_target_pairs={{32,0},{64,32},{96,64},{128,96},{160,128},{192,160},{224,192},{256... | collective-permute-start | bytes 393224 | tf_op jit(solution)/shard_map/while/body/eval_jaxpr/ppermute | solution.py:23
  616.8 13.5 %collective-permute-start.1 = (f32[256,128]{1,0:T(8,128)S(1)}, f32[256,128]{1,0:T(8,128)S(1)}, u32[]{:S(2)}, u32[]{:S(2)}) collective-permute-start(f32[256,128]{1,0:T(8,128)S(1)} %slice.110), channel_id=1, source_target_pairs={{0,32},{32,64},{64,96},{96,128},{128,160},{160,192},{192,224},{224... | collective-permute-start | bytes 393224 | tf_op jit(solution)/shard_map/while/body/eval_jaxpr/ppermute | solution.py:23
  631.3 18.2 %collective-permute-start = (f32[256,128]{1,0:T(8,128)S(1)}, f32[256,128]{1,0:T(8,128)S(1)}, u32[]{:S(2)}, u32[]{:S(2)}) collective-permute-start(f32[256,128]{1,0:T(8,128)S(1)} %get-tuple-element.967), channel_id=1, source_target_pairs={{32,0},{64,32},{96,64},{128,96},{160,128},{192,160},{224,192},{256... | collective-permute-start | bytes 393224 | tf_op jit(solution)/shard_map/while/body/eval_jaxpr/ppermute | solution.py:23
  651.1 13.8 %collective-permute-start.1 = (f32[256,128]{1,0:T(8,128)S(1)}, f32[256,128]{1,0:T(8,128)S(1)}, u32[]{:S(2)}, u32[]{:S(2)}) collective-permute-start(f32[256,128]{1,0:T(8,128)S(1)} %slice.110), channel_id=1, source_target_pairs={{0,32},{32,64},{64,96},{96,128},{128,160},{160,192},{192,224},{224... | collective-permute-start | bytes 393224 | tf_op jit(solution)/shard_map/while/body/eval_jaxpr/ppermute | solution.py:23
  665.9 17.8 %collective-permute-start = (f32[256,128]{1,0:T(8,128)S(1)}, f32[256,128]{1,0:T(8,128)S(1)}, u32[]{:S(2)}, u32[]{:S(2)}) collective-permute-start(f32[256,128]{1,0:T(8,128)S(1)} %get-tuple-element.967), channel_id=1, source_target_pairs={{32,0},{64,32},{96,64},{128,96},{160,128},{192,160},{224,192},{256... | collective-permute-start | bytes 393224 | tf_op jit(solution)/shard_map/while/body/eval_jaxpr/ppermute | solution.py:23
  685.4 14.1 %collective-permute-start.1 = (f32[256,128]{1,0:T(8,128)S(1)}, f32[256,128]{1,0:T(8,128)S(1)}, u32[]{:S(2)}, u32[]{:S(2)}) collective-permute-start(f32[256,128]{1,0:T(8,128)S(1)} %slice.110), channel_id=1, source_target_pairs={{0,32},{32,64},{64,96},{96,128},{128,160},{160,192},{192,224},{224... | collective-permute-start | bytes 393224 | tf_op jit(solution)/shard_map/while/body/eval_jaxpr/ppermute | solution.py:23
  700.4 17.7 %collective-permute-start = (f32[256,128]{1,0:T(8,128)S(1)}, f32[256,128]{1,0:T(8,128)S(1)}, u32[]{:S(2)}, u32[]{:S(2)}) collective-permute-start(f32[256,128]{1,0:T(8,128)S(1)} %get-tuple-element.967), channel_id=1, source_target_pairs={{32,0},{64,32},{96,64},{128,96},{160,128},{192,160},{224,192},{256... | collective-permute-start | bytes 393224 | tf_op jit(solution)/shard_map/while/body/eval_jaxpr/ppermute | solution.py:23
  719.7 14.4 %collective-permute-start.1 = (f32[256,128]{1,0:T(8,128)S(1)}, f32[256,128]{1,0:T(8,128)S(1)}, u32[]{:S(2)}, u32[]{:S(2)}) collective-permute-start(f32[256,128]{1,0:T(8,128)S(1)} %slice.110), channel_id=1, source_target_pairs={{0,32},{32,64},{64,96},{96,128},{128,160},{160,192},{192,224},{224... | collective-permute-start | bytes 393224 | tf_op jit(solution)/shard_map/while/body/eval_jaxpr/ppermute | solution.py:23
  735.0 6.4 collective-permute-start
  753.2 3.2 collective-permute-start.1
  757.3 0.7 copy-start
Sparse Core Ops, SparseCore 0:
  12.3 87.2 all-gather.4
  102.7 100.9 all-gather.2
  210.8 80.0 all-gather.4
  293.9 100.9 all-gather.2
